TPU v7x, 32 devices: a whole 2x2x4 slice. The times are simulated.
32 devices in a mesh: parts: 2 (over y), shard: 2 (over core), blk: 8 (over z, x).
Axes of the slice: x: 2, y: 2, z: 4, core: 2. Of those that a mesh axis runs over, the one named last changes fastest.
Arguments:
- queries_in: bfloat16 [4096, 1024], P(('parts', 'shard', 'blk')), parts along dimension 0, may hold values from -12 to 12
- query_weight: bfloat16 [1024, 1024], replicated, may hold values from -0.1875 to 0.1875
- bank: bfloat16 [2048, 1024], P(('parts', 'shard', 'blk')), parts along dimension 0, may hold values from -110 to 110
- uses: int32 [4096, 2], P(('parts', 'shard', 'blk')), parts along dimension 0, may hold values from 0 to 1, as said below
Outputs:
- retrieved: bfloat16 [4096, 1024], P(('parts', 'shard', 'blk')), parts along dimension 0
There are 2 independent parts, one for each index of `parts`. A program takes and returns all parts, laid end to end along the dimension named above; an argument that names none is the same for every part. Nothing has to cross between parts.
Inputs may be any that keep to these rules, and one draw needn't show every extreme that they name: `uses`: every query lists one or both of the two shards. Of the 128 queries of one device, at most 128 list one shard, and in every draw for every index of blk the queries of both devices at that index all list one same shard.
All inputs are finite; a program needn't handle non-finite values.
Results may differ from a plain program's by a relative error of at most 0.035.
Values may be sent and summed in bfloat16 or wider, within the bound.
A program may use at most 128 MiB of HBM per device.

v0:
```python
import math

import jax
import jax.numpy as jnp
from jax import lax
from jax.sharding import PartitionSpec as P

HEADS = 8
HEAD_DIM = 128


NEGATIVE = -1e30


def empty_carry(slot_count):
    return (
        jnp.full((slot_count, HEADS), NEGATIVE, jnp.float32),
        jnp.zeros((slot_count, HEADS), jnp.float32),
        jnp.zeros((slot_count, HEADS, HEAD_DIM), jnp.float32),
    )


def fold_piece(carry, query_heads, piece, allowed):
    slot_count = query_heads.shape[0]
    piece_rows = piece.shape[0]
    key_rows = math.gcd(piece_rows, 512)
    key_blocks = piece_rows // key_rows
    keys_blocked = piece.reshape(key_blocks, key_rows, HEADS, HEAD_DIM)
    mask_blocked = allowed.reshape(slot_count, key_blocks, key_rows).transpose(1, 0, 2)
    block_rows = math.gcd(slot_count, 128)
    blocks = slot_count // block_rows
    logit_scale = HEAD_DIM ** (-0.5)

    def blocked(array):
        return array.reshape((blocks, block_rows) + array.shape[1:])

    def key_step(state, inputs):
        keys_piece, mask_all = inputs

        def one_block(block_inputs):
            query_block, mask_block, top_old, total_old, accum_old = block_inputs
            scores = (
                jnp.einsum(
                    "shd,rhd->shr", query_block, keys_piece, preferred_element_type=jnp.float32
                )
                * logit_scale
            )
            scores = jnp.where(mask_block[:, None, :], scores, NEGATIVE)
            top_new = jnp.maximum(top_old, jnp.max(scores, axis=-1))
            weights = jnp.where(mask_block[:, None, :], jnp.exp(scores - top_new[..., None]), 0.0)
            factor = jnp.exp(top_old - top_new)
            total_new = total_old * factor + jnp.sum(weights, axis=-1)
            accum_new = accum_old * factor[..., None] + jnp.einsum(
                "shr,rhd->shd",
                weights.astype(jnp.bfloat16),
                keys_piece,
                preferred_element_type=jnp.float32,
            )
            return (top_new, total_new, accum_new)

        top_old, total_old, accum_old = state
        results = lax.map(
            one_block,
            (
                blocked(query_heads),
                blocked(mask_all),
                blocked(top_old),
                blocked(total_old),
                blocked(accum_old),
            ),
        )
        return (
            tuple((result.reshape((slot_count,) + result.shape[2:]) for result in results)),
            None,
        )

    final, unused = lax.scan(key_step, carry, (keys_blocked, mask_blocked))
    return final


def local(queries_in, query_weight, bank, uses):
    row_count = queries_in.shape[0]
    width_all = HEADS * HEAD_DIM
    projected = jnp.dot(queries_in, query_weight, preferred_element_type=jnp.float32).astype(
        jnp.bfloat16
    )
    positions = jnp.cumsum(uses, axis=0) - 1
    listed = uses > 0
    onehot_table = (positions.T[:, None, :] == jnp.arange(row_count)[None, :, None]) & listed.T[
        :, None, :
    ]
    outgoing = jnp.einsum(
        "sct,td->scd",
        onehot_table.astype(jnp.bfloat16),
        projected,
        preferred_element_type=jnp.float32,
    ).astype(jnp.bfloat16)
    incoming = lax.all_to_all(outgoing, "shard", split_axis=0, concat_axis=0, tiled=True)
    item_count = incoming.shape[1]
    slot_heads = incoming.reshape(2 * item_count, HEADS, HEAD_DIM)
    piece = lax.all_gather(bank, "blk", axis=0, tiled=True)
    allowed = jnp.ones((2 * item_count, piece.shape[0]), dtype=jnp.bool_)
    top_part, total_part, accum_part = fold_piece(
        empty_carry(2 * item_count), slot_heads, piece, allowed
    )
    accum_back = lax.all_to_all(
        accum_part.reshape(2, item_count, width_all).astype(jnp.bfloat16),
        "shard",
        split_axis=0,
        concat_axis=0,
        tiled=True,
    ).astype(jnp.float32)
    top_back = lax.all_to_all(
        top_part.reshape(2, item_count, HEADS).astype(jnp.bfloat16),
        "shard",
        split_axis=0,
        concat_axis=0,
        tiled=True,
    ).astype(jnp.float32)
    total_back = lax.all_to_all(
        total_part.reshape(2, item_count, HEADS).astype(jnp.bfloat16),
        "shard",
        split_axis=0,
        concat_axis=0,
        tiled=True,
    ).astype(jnp.float32)
    safe_slot = jnp.clip(positions, 0, row_count - 1)
    top_pair = jnp.stack(
        [jnp.take(top_back[member], safe_slot[:, member], axis=0) for member in range(2)], 1
    )
    total_pair = jnp.stack(
        [jnp.take(total_back[member], safe_slot[:, member], axis=0) for member in range(2)], 1
    )
    accum_pair = jnp.stack(
        [jnp.take(accum_back[member], safe_slot[:, member], axis=0) for member in range(2)], 1
    )
    accum_pair = accum_pair.reshape(row_count, 2, HEADS, HEAD_DIM)
    top_pair = jnp.where(listed[:, :, None], top_pair, NEGATIVE)
    highest = jnp.max(top_pair, axis=1)
    scale_pair = jnp.where(listed[:, :, None], jnp.exp(top_pair - highest[:, None, :]), 0.0)
    total_all = jnp.sum(scale_pair * total_pair, axis=1)
    accum_all = jnp.sum(scale_pair[..., None] * accum_pair, axis=1)
    return (accum_all / total_all[..., None]).reshape(row_count, width_all).astype(jnp.bfloat16)


def solution(mesh):
    in_specs = (
        P(("parts", "shard", "blk"), None),
        P(),
        P(("parts", "shard", "blk"), None),
        P(("parts", "shard", "blk"), None),
    )
    out_specs = P(("parts", "shard", "blk"), None)
    return jax.shard_map(local, mesh=mesh, in_specs=in_specs, out_specs=out_specs, check_vma=False)
```

profile of v0, /device:TPU:1, one launch (start us, length us, event | category | flops | bytes accessed | tf_op | source)
XLA Modules:
  0.0 94.7 jit_solution(11347580435513448345)
XLA Ops:
  6.5 0.7 all-gather.2.cloned.1.call-update
  7.3 0.8 copy.41
  8.4 2.4 %convolution_convert_fusion = bf16[2,128,1024]{2,1,0:T(8,128)(2,1)} fusion(bf16[128,1024]{1,0:T(8,128)(2,1)} %param.10, bf16[1024,1024]{1,0:T(8,128)(2,1)S(1)} %copy-done, s32[2,128]{1,0:T(2,128)S(1)} %copy.44, pred[2,128]{1,0:T(4,128)(4,1)S(1)} %copy.45), kind=kOutput, calls=%fused_computation.29 | convolution fusion | flops 336003072 | bytes 2884864 | tf_op jit(solution)/shard_map/sct,td->scd/dot_general | solution.py:92
  10.8 3.5 %all-to-all-start = ((bf16[2,128,1024]{2,1,0:T(8,128)(2,1)}), bf16[2,128,1024]{2,1,0:T(8,128)(2,1)S(1)}, u32[]{:S(2)}, u32[]{:S(2)}) async-start(bf16[2,128,1024]{2,1,0:T(8,128)(2,1)} %convolution_convert_fusion), calls=%async_computation | async-start | bytes 1048576 | tf_op jit(solution)/shard_map/all_to_all | solution.py:98
  14.5 1.3 %all-to-all-done = bf16[2,128,1024]{2,1,0:T(8,128)(2,1)S(1)} async-done(((bf16[2,128,1024]{2,1,0:T(8,128)(2,1)}), bf16[2,128,1024]{2,1,0:T(8,128)(2,1)S(1)}, u32[]{:S(2)}, u32[]{:S(2)}) %all-to-all-start) | async-done | bytes 524320 | tf_op jit(solution)/shard_map/all_to_all | solution.py:98
  15.7 0.9 copy.60
  16.9 33.9 %all-gather.2.cloned.1.call-done = bf16[512,1024]{1,0:T(8,128)(2,1)} async-done(((bf16[64,1024]{1,0:T(8,128)(2,1)}), bf16[512,1024]{1,0:T(8,128)(2,1)}) %all-gather.2.cloned.1.call-update) | async-done | bytes 1048592 | tf_op jit(solution)/shard_map/all_gather | solution.py:101
  50.8 2.3 %copy.46 = bf16[512,1024]{0,1:T(8,128)(2,1)} copy(bf16[512,1024]{1,0:T(8,128)(2,1)} %all-gather.2.cloned.1.call-done) | data formatting | bytes 2097152 | tf_op jit(solution)/shard_map/all_gather | solution.py:101
  53.1 1.6 %copy.48 = bf16[512,8,128]{2,0,1:T(8,128)(2,1)S(1)} copy(bf16[512,8,128]{0,2,1:T(8,128)(2,1)} %bitcast.121) | data formatting | bytes 2097152 | tf_op jit(solution)/shard_map/while/body/eval_jaxpr/while | solution.py:62
  54.7 7.4 %while.26 = (s32[]{:T(128)}, bf16[2,128,8]{1,2,0:T(8,128)(2,1)S(1)}, bf16[2,128,8]{1,2,0:T(8,128)(2,1)}, bf16[2,128,8,128]{3,1,2,0:T(8,128)(2,1)}, bf16[2,128,8,...) while((s32[]{:T(128)}, bf16[2,128,8]{1,2,0:T(8,128)(2,1)S(1)}, ...), condition=%wide.region_4.5_spmd, body=%wide.region_1.4_spmd.sunk | while | flops 272768000 | bytes 13944989 | solution.py:62
  54.7 1.0 %constant_dynamic-slice_fusion.2 = bf16[1,128,8,128]{3,2,1,0:T(8,128)(2,1)S(1)} fusion(bf16[2,128,8,128]{3,2,1,0:T(8,128)(2,1)} %get-tuple-element.220, s32[]{:T(128)S(6)} %copy.80), kind=kLoop, calls=%fused_computation.27.clone.1 | loop fusion | bytes 524292 | tf_op jit(solution)/shard_map/while/body/eval_jaxpr/while/body/jit(dynamic_index_in_dim)/dynamic_slice | solution.py:62
  56.2 0.6 fusion.37
  56.8 0.7 fusion.39
  57.6 0.7 fusion.38
  58.4 1.0 %constant_dynamic-slice_fusion.2 = bf16[1,128,8,128]{3,2,1,0:T(8,128)(2,1)S(1)} fusion(bf16[2,128,8,128]{3,2,1,0:T(8,128)(2,1)} %get-tuple-element.220, s32[]{:T(128)S(6)} %copy.80), kind=kLoop, calls=%fused_computation.27.clone.1 | loop fusion | bytes 524292 | tf_op jit(solution)/shard_map/while/body/eval_jaxpr/while/body/jit(dynamic_index_in_dim)/dynamic_slice | solution.py:62
  60.5 0.7 fusion.39
  61.3 0.7 fusion.38
  62.1 1.9 %copy_bitcast_fusion.2 = bf16[2,128,1024]{2,1,0:T(8,128)(2,1)} fusion(bf16[2,128,8,128]{3,1,2,0:T(8,128)(2,1)} %get-tuple-element.95), kind=kLoop, calls=%fused_computation.34 | loop fusion | bytes 1048576 | tf_op jit(solution)/shard_map/convert_element_type | solution.py:107
  64.0 5.0 %all_to_all.20 = bf16[2,128,8]{1,2,0:T(8,128)(2,1)S(1)} all-to-all(bf16[2,128,8]{1,2,0:T(8,128)(2,1)S(1)} %get-tuple-element.94), channel_id=1, replica_groups=mesh['parts'=2,'shard'=2,'blk'=8] {'shard'}, dimensions={0} | all-to-all | bytes 8192 | tf_op jit(solution)/shard_map/all_to_all | solution.py:113
  69.0 3.5 %all-to-all-start.3 = ((bf16[2,128,8]{1,2,0:T(8,128)(2,1)}), bf16[2,128,8]{1,2,0:T(8,128)(2,1)S(1)}, u32[]{:S(2)}, u32[]{:S(2)}) async-start(bf16[2,128,8]{1,2,0:T(8,128)(2,1)} %get-tuple-element.96), calls=%async_computation.3 | async-start | bytes 8192 | tf_op jit(solution)/shard_map/all_to_all | solution.py:120
  72.7 0.9 all-to-all-done.3
  73.6 3.8 %all-to-all-start.2 = ((bf16[2,128,1024]{2,1,0:T(8,128)(2,1)}), bf16[2,128,1024]{2,1,0:T(8,128)(2,1)S(1)}, u32[]{:S(2)}, u32[]{:S(2)}) async-start(bf16[2,128,1024]{2,1,0:T(8,128)(2,1)} %copy_bitcast_fusion.2), calls=%async_computation.2 | async-start | bytes 1048576 | tf_op jit(solution)/shard_map/all_to_all | solution.py:106
  77.5 0.6 gather_fusion
  78.2 0.6 gather_fusion.4
  79.0 0.7 gather_fusion.1
  79.7 0.6 gather_fusion.5
  81.0 1.6 %gather_fusion.2 = f32[128,1024]{1,0:T(8,128)} fusion(f32[128,1024]{1,0:T(8,128)S(1)} %get-tuple-element.141, s32[1024]{0:T(1024)S(1)} %pad_clamp_fusion.1), kind=kCustom, calls=%fused_computation.1.clone | custom fusion | bytes 1049088 | tf_op jit(solution)/shard_map/jit(_take)/gather | solution.py:135
  82.6 1.1 %select_bitcast_fusion.1 = f32[16,8,8,128]{3,1,2,0:T(8,128)S(1)} fusion(f32[128,1024]{1,0:T(8,128)} %gather_fusion.2, pred[128]{0:T(512)(128)(4,1)S(1)} %get-tuple-element.156), kind=kLoop, calls=%fused_computation.38 | loop fusion | flops 131072 | bytes 1048704
  83.8 0.9 copy.61
  84.7 0.8 gather_fusion.3
  85.7 0.8 copy-done.1
  87.1 0.8 copy.70
  (57 shorter events, 4.5 us)
Async XLA Ops:
  6.5 1.9 %copy-start = (bf16[1024,1024]{1,0:T(8,128)(2,1)S(1)}, bf16[1024,1024]{1,0:T(8,128)(2,1)}, u32[]{:S(2)}) copy-start(bf16[1024,1024]{1,0:T(8,128)(2,1)} %param.11) | copy-start | bytes 6291460
  6.5 44.3 %all-gather.2.cloned.1.call-start = ((), (), s32[]{:S(2)}) async-start(), calls=%async_computation.4 | async-start | bytes 1179648 | tf_op jit(solution)/shard_map/all_gather | solution.py:101
  10.8 4.9 %all-to-all-start = ((bf16[2,128,1024]{2,1,0:T(8,128)(2,1)}), bf16[2,128,1024]{2,1,0:T(8,128)(2,1)S(1)}, u32[]{:S(2)}, u32[]{:S(2)}) async-start(bf16[2,128,1024]{2,1,0:T(8,128)(2,1)} %convolution_convert_fusion), calls=%async_computation | async-start | bytes 1048576 | tf_op jit(solution)/shard_map/all_to_all | solution.py:98
  55.7 1.1 %copy-start.2 = (bf16[2,128,8,128]{3,1,2,0:T(8,128)(2,1)S(1)}, bf16[2,128,8,128]{3,1,2,0:T(8,128)(2,1)}, u32[]{:S(2)}) copy-start(bf16[2,128,8,128]{3,1,2,0:T(8,128)(2,1)} %get-tuple-element.212) | copy-start | bytes 1572868 | tf_op jit(solution)/shard_map/while/body/eval_jaxpr/while
  57.6 0.8 copy-start.3
  59.4 1.1 %copy-start.2 = (bf16[2,128,8,128]{3,1,2,0:T(8,128)(2,1)S(1)}, bf16[2,128,8,128]{3,1,2,0:T(8,128)(2,1)}, u32[]{:S(2)}) copy-start(bf16[2,128,8,128]{3,1,2,0:T(8,128)(2,1)} %get-tuple-element.212) | copy-start | bytes 1572868 | tf_op jit(solution)/shard_map/while/body/eval_jaxpr/while
  61.3 0.8 copy-start.3
  69.0 4.6 %all-to-all-start.3 = ((bf16[2,128,8]{1,2,0:T(8,128)(2,1)}), bf16[2,128,8]{1,2,0:T(8,128)(2,1)S(1)}, u32[]{:S(2)}, u32[]{:S(2)}) async-start(bf16[2,128,8]{1,2,0:T(8,128)(2,1)} %get-tuple-element.96), calls=%async_computation.3 | async-start | bytes 8192 | tf_op jit(solution)/shard_map/all_to_all | solution.py:120
  73.6 7.3 %all-to-all-start.2 = ((bf16[2,128,1024]{2,1,0:T(8,128)(2,1)}), bf16[2,128,1024]{2,1,0:T(8,128)(2,1)S(1)}, u32[]{:S(2)}, u32[]{:S(2)}) async-start(bf16[2,128,1024]{2,1,0:T(8,128)(2,1)} %copy_bitcast_fusion.2), calls=%async_computation.2 | async-start | bytes 1048576 | tf_op jit(solution)/shard_map/all_to_all | solution.py:106
  85.5 1.0 %copy-start.1 = (f32[16,8,8,128]{3,2,1,0:T(8,128)S(1)}, f32[16,8,8,128]{3,2,1,0:T(8,128)}, u32[]{:S(2)}) copy-start(f32[16,8,8,128]{3,2,1,0:T(8,128)} %copy.61) | copy-start | bytes 1572868
Sparse Core Ops, SparseCore 0:
  9.5 41.2 all-gather.1
where the time goes:
time: 95.3 us; the launch traced here: 94.7 us
  waiting for transfers between devices  36.8 us (39%)
  local copies, waits for them, and re-layouts  18.4 us (19%)
  between operations  13.6 us (14%)
  starting transfers between devices  10.9 us (11%)
  blocking collectives  5.01 us (5%)
  matrix products  4.94 us (5%)
  other arithmetic  4.87 us (5%)
    all_gather x1, waiting for transfers between devices, local(): piece = lax.all_gather(bank, 'blk', axis=0, tiled=True)  33.9 us
    all_to_all x1, blocking collectives, local(): lax.all_to_all(top_part.reshape(2, item_count, HEADS).astype(jnp.bfloat16...  5.01 us
    unnamed x9, local copies, waits for them, and re-layouts  4.23 us
    all_to_all x1, starting transfers between devices, local(): lax.all_to_all(accum_part.reshape(2, item_count, width_all).astype(jnp.bf...  3.81 us
    all_to_all x1, starting transfers between devices, local(): lax.all_to_all(total_part.reshape(2, item_count, HEADS).astype(jnp.bfloat...  3.55 us
    all_to_all x1, starting transfers between devices, local(): lax.all_to_all(outgoing, 'shard', split_axis=0, concat_axis=0, tiled=True)  3.53 us
    dot_general x1, matrix products, local(): jnp.einsum('sct,td->scd', onehot_table.astype(jnp.bfloat16), projected, p...  2.43 us
    gather x2, local copies, waits for them, and re-layouts, local(): jnp.take(accum_back[member], safe_slot[:, member], axis=0)  2.38 us
  transfers between devices with their start and end apart: 4, of which 3 were waited for; matrix products, arithmetic and copies ran while one was open for 9% of the time, Pallas kernels for 0%

commit v1 on v0

v1 whole, which is shorter than its diff:
```python
import math

import jax
import jax.numpy as jnp
from jax import lax
from jax.sharding import PartitionSpec as P

HEADS = 8
HEAD_DIM = 128
NEGATIVE = -1e30


def local_xla(queries_in, query_weight, bank, uses):
    rows = queries_in.shape[0]
    projected = jnp.dot(queries_in, query_weight, preferred_element_type=jnp.float32).astype(
        jnp.bfloat16
    )
    heads = projected.reshape(rows, HEADS, HEAD_DIM)
    whole = lax.all_gather(bank, ("shard", "blk"), axis=0, tiled=True)
    shard_rows = whole.shape[0] // 2
    chunk_rows = math.gcd(shard_rows, 512)
    chunks = shard_rows // chunk_rows
    blocked = whole.reshape(2, chunks, chunk_rows, HEADS, HEAD_DIM)
    allowed = uses > 0

    def step(carry, keys):
        top_old, total_old, accum_old = carry
        scores = jnp.einsum("thd,srhd->htsr", heads, keys, preferred_element_type=jnp.float32)
        scores = jnp.where(allowed[None, :, :, None], scores * HEAD_DIM**-0.5, NEGATIVE)
        top = jnp.maximum(top_old, jnp.max(scores, axis=(2, 3)))
        weights = jnp.exp(scores - top[:, :, None, None])
        factor = jnp.exp(top_old - top)
        total = total_old * factor + jnp.sum(weights, axis=(2, 3))
        accum = accum_old * factor[..., None] + jnp.einsum(
            "htsr,srhd->htd",
            weights.astype(jnp.bfloat16),
            keys,
            preferred_element_type=jnp.float32,
        )
        return (top, total, accum), None

    start = (
        jnp.full((HEADS, rows), NEGATIVE, jnp.float32),
        jnp.zeros((HEADS, rows), jnp.float32),
        jnp.zeros((HEADS, rows, HEAD_DIM), jnp.float32),
    )
    (top, total, accum), _ = lax.scan(step, start, blocked.transpose(1, 0, 2, 3, 4))
    out = (accum / total[..., None]).astype(jnp.bfloat16)
    return out.transpose(1, 0, 2).reshape(rows, HEADS * HEAD_DIM)


def solution(mesh):
    spec = P(("parts", "shard", "blk"), None)
    return jax.shard_map(
        local_xla, mesh=mesh, in_specs=(spec, P(), spec, spec), out_specs=spec, check_vma=False
    )
```

time: 95.3 us -> 74.7 us (0.78)
  starting transfers between devices: 10.9 us -> 0.01 us
  local copies, waits for them, and re-layouts: 18.4 us -> 9.69 us
  waiting for transfers between devices: 36.8 us -> 43.9 us
  blocking collectives: 5.01 us -> 0 us
  other arithmetic: 4.87 us -> 1.8 us
    all_to_all x3 -> x0, starting transfers between devices: 10.9 us -> none  [the longest x1 3.81 us: local(): lax.all_to_all(accum_part.reshape(2, item_count, width_all).astype(jnp.bf...]
    all_gather x1, waiting for transfers between devices: 33.9 us -> 43.2 us  [local_xla(): whole = lax.all_gather(bank, ('shard', 'blk'), axis=0, tiled=True)]
    all_to_all x1 -> x0, blocking collectives: 5.01 us -> none  [local(): lax.all_to_all(top_part.reshape(2, item_count, HEADS).astype(jnp.bfloat16...]
    gather x6 -> x0, local copies, waits for them, and re-layouts: 4.98 us -> none  [the longest x2 2.38 us: local(): jnp.take(accum_back[member], safe_slot[:, member], axis=0)]
    squeeze x3 -> x1, local copies, waits for them, and re-layouts: 0.09 us -> 4.36 us  [local_xla(): lax.scan(step, start, blocked.transpose(1, 0, 2, 3, 4))]
    all_gather x1 -> x0, local copies, waits for them, and re-layouts: 2.28 us -> none  [local(): piece = lax.all_gather(bank, 'blk', axis=0, tiled=True)]
    all_to_all x3 -> x0, waiting for transfers between devices: 2.15 us -> none  [the longest x1 1.28 us: local(): lax.all_to_all(outgoing, 'shard', split_axis=0, concat_axis=0, tiled=True)]
    dynamic_slice x2 -> x0, local copies, waits for them, and re-layouts: 1.94 us -> none  [key_step(): lax.map(one_block, (blocked(query_heads), blocked(mask_all), blocked(top_...]
  transfers between devices with their start and end apart: 4 -> 1, of which waited for: 3 -> 1; matrix products, arithmetic and copies ran while one was open for 9% -> 3% of each run, Pallas kernels for 0% -> 0%
where the time goes in v1:
time: 74.7 us; the launch traced here: 74.3 us
  waiting for transfers between devices  43.9 us (59%)
  between operations  13.4 us (18%)
  local copies, waits for them, and re-layouts  9.69 us (13%)
  matrix products  5.39 us (7%)
  other arithmetic  1.8 us (2%)
    all_gather x1, waiting for transfers between devices, local_xla(): whole = lax.all_gather(bank, ('shard', 'blk'), axis=0, tiled=True)  43.2 us
    unnamed x6, local copies, waits for them, and re-layouts  4.48 us
    squeeze x1, local copies, waits for them, and re-layouts, local_xla(): lax.scan(step, start, blocked.transpose(1, 0, 2, 3, 4))  4.36 us
    dot_general x1, matrix products, step(): jnp.einsum('thd,srhd->htsr', heads, keys, preferred_element_type=jnp.floa...  2.65 us
  transfers between devices with their start and end apart: 1, of which 1 were waited for; matrix products, arithmetic and copies ran while one was open for 3% of the time, Pallas kernels for 0%

profile of v1, /device:TPU:1, one launch (start us, length us, event | category | flops | bytes accessed | tf_op | source)
XLA Modules:
  0.0 74.3 jit_solution(16575719060348413938)
XLA Ops:
  6.5 0.0 copy-start
  6.5 0.0 all-gather.2.cloned.1.call-start
  6.5 0.7 all-gather.2.cloned.1.call-update
  7.3 0.9 %copy-done = bf16[1024,1024]{1,0:T(8,128)(2,1)S(1)} copy-done((bf16[1024,1024]{1,0:T(8,128)(2,1)S(1)}, bf16[1024,1024]{1,0:T(8,128)(2,1)}, u32[]{:S(2)}) %copy-start) | copy-done | bytes 2097176
  8.1 1.4 %fusion.15 = bf16[16,8,8,128]{3,1,2,0:T(8,128)(2,1)S(1)} fusion(bf16[128,1024]{1,0:T(8,128)(2,1)} %param.4, bf16[1024,1024]{1,0:T(8,128)(2,1)S(1)} %copy-done), kind=kOutput, calls=%fused_computation.13 | convolution fusion | flops 268566528 | bytes 2621440 | tf_op jit(solution)/shard_map/dot_general | solution.py:15
  9.6 0.7 broadcast_compare_fusion
  10.3 43.2 %all-gather.2.cloned.1.call-done = bf16[1024,1024]{1,0:T(8,128)(2,1)} async-done(((bf16[64,1024]{1,0:T(8,128)(2,1)}), bf16[1024,1024]{1,0:T(8,128)(2,1)}) %all-gather.2.cloned.1.call-update) | async-done | bytes 2097168 | tf_op jit(solution)/shard_map/all_gather | solution.py:19
  53.5 3.6 %copy.17 = bf16[128,8,8,128]{3,2,1,0:T(8,128)(2,1)} copy(bf16[128,8,8,128]{3,1,2,0:T(8,128)(2,1)} %bitcast.31) | data formatting | bytes 4194304
  57.1 4.4 %copy.10 = bf16[2,512,8,128]{1,3,0,2:T(8,128)(2,1)} copy(bf16[2,512,8,128]{3,2,1,0:T(8,128)(2,1)} %bitcast.30) | data formatting | bytes 4194304 | tf_op jit(solution)/shard_map/while/body/jit(dynamic_index_in_dim)/squeeze | solution.py:47
  61.4 0.0 copy-start.1
  61.4 2.7 %fusion = (f32[8,128]{1,0:T(8,128)S(1)}, f32[8,128,2,512]{3,1,2,0:T(8,128)S(1)}) fusion(pred[128,2]{0,1:T(4,128)(4,1)S(1)} %broadcast_compare_fusion, bf16[2,512,8,128]{1,3,0,2:T(8,128)(2,1)} %copy.10, bf16[128,8,128,1]{2,1,0,3:T(8,128)(2,1)S(1)} %bitcast.32), kind=kOutput, calls=%fused_computation.2 | convolution fusion | flops 271580160 | bytes 6557952 | tf_op jit(solution)/shard_map/while/body/eval_jaxpr/thd,srhd->htsr/dot_general | solution.py:28
  64.1 1.1 %fusion.1 = f32[8,128]{1,0:T(8,128)S(1)} fusion(f32[8,128,2,512]{3,1,2,0:T(8,128)S(1)} %get-tuple-element.20, f32[8,128]{1,0:T(8,128)S(1)} %get-tuple-element.18, pred[128,2]{0,1:T(4,128)(4,1)S(1)} %broadcast_compare_fusion), kind=kLoop, calls=%fused_computation.3 | loop fusion | flops 4193280 | bytes 4202752 | tf_op jit(solution)/shard_map/while/body/eval_jaxpr/reduce_sum | solution.py:33
  65.2 0.0 copy-done.1
  65.2 1.3 %fusion.19 = bf16[128,8,128]{0,2,1:T(8,128)(2,1)S(1)} fusion(bf16[2,512,8,128]{1,3,0,2:T(8,128)(2,1)S(1)} %copy-done.1, f32[8,128,2,512]{3,1,2,0:T(8,128)S(1)} %get-tuple-element.20, f32[8,128]{1,0:T(8,128)S(1)} %get-tuple-element.18, pred[128,2]{0,1:T(4,128)(4,1)S(1)} %broadcast_compare_fusion, f32[128,8]{0,1:T(8,128)S(1)} %bitcast_add_fusion, ...), kind=kOutput, calls=%fused_computation.15 | convolution fusion | flops 273022976 | bytes 6566144 | tf_op jit(solution)/shard_map/while/body/eval_jaxpr/htsr,srhd->htd/dot_general | solution.py:34
  66.6 0.9 %copy.11 = bf16[128,1024]{1,0:T(8,128)(2,1)} copy(bf16[128,1024]{0,1:T(8,128)(2,1)S(1)} %bitcast.33) | data formatting | bytes 524288 | tf_op jit(solution)/shard_map/reshape | solution.py:49
  (3 shorter events, 0.1 us)
Async XLA Ops:
  6.5 1.6 %copy-start = (bf16[1024,1024]{1,0:T(8,128)(2,1)S(1)}, bf16[1024,1024]{1,0:T(8,128)(2,1)}, u32[]{:S(2)}) copy-start(bf16[1024,1024]{1,0:T(8,128)(2,1)} %param.5) | copy-start | bytes 6291460
  6.5 47.0 %all-gather.2.cloned.1.call-start = ((), (), s32[]{:S(2)}) async-start(), calls=%async_computation | async-start | bytes 2228224 | tf_op jit(solution)/shard_map/all_gather | solution.py:19
  61.4 3.8 %copy-start.1 = (bf16[2,512,8,128]{1,3,0,2:T(8,128)(2,1)S(1)}, bf16[2,512,8,128]{1,3,0,2:T(8,128)(2,1)}, u32[]{:S(2)}) copy-start(bf16[2,512,8,128]{1,3,0,2:T(8,128)(2,1)} %copy.10) | copy-start | bytes 6291460
Sparse Core Ops, SparseCore 0:
  9.6 43.8 all-gather.1

commit v2 on v1

--- a/solution.py
+++ b/solution.py
@@ -1,13 +1,216 @@
+import functools
 import math
 
 import jax
 import jax.numpy as jnp
 from jax import lax
+from jax.experimental import pallas as pl
+from jax.experimental.pallas import tpu as pltpu
 from jax.sharding import PartitionSpec as P
 
 HEADS = 8
 HEAD_DIM = 128
 NEGATIVE = -1e30
+ALONG_X = 2
+MESH = pl.DeviceIdType.MESH
+
+
+def kernel(
+    depth,
+    queries_hbm,
+    weight_hbm,
+    bank_hbm,
+    uses_ref,
+    out_ref,
+    held,
+    queries_ref,
+    weight_ref,
+    projected,
+    top_ref,
+    total_ref,
+    accum_ref,
+    load_sems,
+    z_sems,
+    x_sems,
+    core_sems,
+    recv_sems,
+):
+    part = lax.axis_index("parts")
+    core = lax.axis_index("shard")
+    blk = lax.axis_index("blk")
+    z, x = blk // ALONG_X, blk % ALONG_X
+    other_x, other_core = 1 - x, 1 - core
+
+    def at(to_core, to_z, to_x):
+        return (part, to_core, to_z * ALONG_X + to_x)
+
+    def copy(of_z, of_core, of_x, sems, target, source=None):
+        slot = held.at[of_z, of_core, of_x]
+        return pltpu.make_async_remote_copy(
+            src_ref=slot if source is None else source,
+            dst_ref=slot,
+            send_sem=sems.at[of_z, of_x],
+            recv_sem=recv_sems.at[of_z, of_core, of_x],
+            device_id=target,
+            device_id_type=MESH,
+        )
+
+    def along(of_z, step, source=None):
+        return copy(of_z, core, x, z_sems.at[0 if step > 0 else 1], at(core, z + step, x), source)
+
+    def across(of_z, source=None):
+        return copy(of_z, core, x, x_sems, at(core, z, other_x), source)
+
+    def over(of_z, of_x, source=None):
+        return copy(of_z, core, of_x, core_sems, at(other_core, z, x), source)
+
+    def arrived(of_z, of_core, of_x):
+        copy(of_z, of_core, of_x, x_sems, at(core, z, other_x)).wait_recv()
+
+    loads = [
+        pltpu.make_async_copy(weight_hbm, weight_ref, load_sems.at[0]),
+        pltpu.make_async_copy(queries_hbm, queries_ref, load_sems.at[1]),
+        pltpu.make_async_copy(bank_hbm, held.at[z, core, x], load_sems.at[2]),
+    ]
+    for load in loads:
+        load.start()
+
+    barrier = pltpu.get_barrier_semaphore()
+    below, above = z > 0, z < depth - 1
+
+    def greet(target):
+        pl.semaphore_signal(barrier, inc=1, device_id=target, device_id_type=MESH)
+
+    greet(at(core, z, other_x))
+    greet(at(other_core, z, x))
+    pl.when(below)(lambda: greet(at(core, z - 1, x)))
+    pl.when(above)(lambda: greet(at(core, z + 1, x)))
+    pl.semaphore_wait(barrier, 2 + below.astype(jnp.int32) + above.astype(jnp.int32))
+
+    pl.when(below)(lambda: along(z, -1, bank_hbm).start())
+    pl.when(above)(lambda: along(z, 1, bank_hbm).start())
+    across(z, bank_hbm).start()
+    over(z, x, bank_hbm).start()
+
+    for load in loads[:2]:
+        load.wait()
+    for head in range(0, HEADS, 2):
+        columns = slice(head * HEAD_DIM, (head + 2) * HEAD_DIM)
+        projected[:, columns] = jnp.dot(
+            queries_ref[...], weight_ref[:, columns], preferred_element_type=jnp.float32
+        ).astype(jnp.bfloat16)
+    loads[2].wait()
+
+    factor = HEAD_DIM**-0.5 * math.log2(math.e)
+    rows = held.shape[3]
+    plane_rows = 2 * ALONG_X * rows
+    rows_q = projected.shape[0]
+
+    def attend(of_z, first):
+        in_second = (
+            lax.broadcasted_iota(jnp.int32, (rows_q, plane_rows), 1) >= ALONG_X * rows
+        )
+        allowed = jnp.where(in_second, uses_ref[:, 1:2], uses_ref[:, 0:1]) > 0
+        for head in range(HEADS):
+            columns = slice(head * HEAD_DIM, (head + 1) * HEAD_DIM)
+            keys = held[of_z, :, :, :, columns].reshape(plane_rows, HEAD_DIM)
+            scores = lax.dot_general(
+                projected[:, columns],
+                keys,
+                (((1,), (1,)), ((), ())),
+                preferred_element_type=jnp.float32,
+            )
+            scores = jnp.where(allowed, scores * factor, NEGATIVE)
+            top = jnp.max(scores, axis=1, keepdims=True)
+            if not first:
+                top_old = top_ref[head]
+                top = jnp.maximum(top_old, top)
+            weights = jnp.exp2(scores - top[:, :1])
+            total = weights[:, :HEAD_DIM]
+            for start in range(HEAD_DIM, plane_rows, HEAD_DIM):
+                total = total + weights[:, start : start + HEAD_DIM]
+            summed = jnp.dot(
+                weights.astype(jnp.bfloat16), keys, preferred_element_type=jnp.float32
+            )
+            if first:
+                top = jnp.broadcast_to(top, (rows_q, HEAD_DIM))
+            else:
+                shrink = jnp.exp2(top_old - top)
+                total = total + total_ref[head] * shrink
+                summed = summed + accum_ref[head] * shrink
+            top_ref[head] = top
+            total_ref[head] = total
+            accum_ref[head] = summed
+
+    def planes(distance, action):
+        if distance == 0:
+            action(z, 0)
+            return
+        pl.when(z >= distance)(lambda: action(z - distance, 1))
+        pl.when(z < depth - distance)(lambda: action(z + distance, -1))
+
+    def relay(of_z, step):
+        arrived(of_z, core, x)
+        pl.when((z + step >= 0) & (z + step < depth))(lambda: along(of_z, step).start())
+        across(of_z).start()
+        over(of_z, x).start()
+
+    def hand_over(of_z, step):
+        arrived(of_z, core, other_x)
+        over(of_z, other_x).start()
+
+    def finish_plane(of_z, step):
+        arrived(of_z, other_core, 0)
+        arrived(of_z, other_core, 1)
+        attend(of_z, step == 0)
+
+    for distance in range(depth):
+        if distance + 1 < depth:
+            planes(distance + 1, relay)
+        planes(distance, hand_over)
+        planes(distance, finish_plane)
+
+    for head in range(HEADS):
+        columns = slice(head * HEAD_DIM, (head + 1) * HEAD_DIM)
+        total = jnp.sum(total_ref[head], axis=1, keepdims=True)
+        out_ref[:, columns] = (accum_ref[head] / total).astype(out_ref.dtype)
+
+    for of_z in range(depth):
+        pl.when((z >= of_z) & above)(lambda of_z=of_z: along(of_z, 1).wait_send())
+        pl.when((z <= of_z) & below)(lambda of_z=of_z: along(of_z, -1).wait_send())
+        across(of_z).wait_send()
+        for of_x in range(ALONG_X):
+            over(of_z, of_x).wait_send()
+
+
+def local_kernel(depth, queries_in, query_weight, bank, uses):
+    rows_q, width = queries_in.shape
+    rows = bank.shape[0]
+    any_space = pl.BlockSpec(memory_space=pl.ANY)
+    return pl.pallas_call(
+        functools.partial(kernel, depth),
+        out_shape=jax.ShapeDtypeStruct((rows_q, HEADS * HEAD_DIM), jnp.bfloat16),
+        in_specs=[any_space, any_space, any_space, pl.BlockSpec(memory_space=pltpu.VMEM)],
+        out_specs=pl.BlockSpec(memory_space=pltpu.VMEM),
+        scratch_shapes=[
+            pltpu.VMEM((depth, 2, ALONG_X, rows, width), jnp.bfloat16),
+            pltpu.VMEM((rows_q, width), jnp.bfloat16),
+            pltpu.VMEM((width, width), jnp.bfloat16),
+            pltpu.VMEM((rows_q, width), jnp.bfloat16),
+            pltpu.VMEM((HEADS, rows_q, HEAD_DIM), jnp.float32),
+            pltpu.VMEM((HEADS, rows_q, HEAD_DIM), jnp.float32),
+            pltpu.VMEM((HEADS, rows_q, HEAD_DIM), jnp.float32),
+            pltpu.SemaphoreType.DMA((3,)),
+            pltpu.SemaphoreType.DMA((2, depth, ALONG_X)),
+            pltpu.SemaphoreType.DMA((depth, ALONG_X)),
+            pltpu.SemaphoreType.DMA((depth, ALONG_X)),
+            pltpu.SemaphoreType.DMA((depth, 2, ALONG_X)),
+        ],
+        compiler_params=pltpu.CompilerParams(
+            collective_id=0, has_side_effects=True, vmem_limit_bytes=32 * 2**20
+        ),
+        name="gather_attend",
+    )(queries_in, query_weight, bank, uses)
 
 
 def local_xla(queries_in, query_weight, bank, uses):
@@ -51,6 +254,8 @@
 
 def solution(mesh):
     spec = P(("parts", "shard", "blk"), None)
+    blocks = mesh.shape["blk"]
+    local = functools.partial(local_kernel, blocks // ALONG_X) if blocks == 8 else local_xla
     return jax.shard_map(
-        local_xla, mesh=mesh, in_specs=(spec, P(), spec, spec), out_specs=spec, check_vma=False
+        local, mesh=mesh, in_specs=(spec, P(), spec, spec), out_specs=spec, check_vma=False
     )

time: 74.7 us -> 29.4 us (0.39)
  waiting for transfers between devices: 43.9 us -> 0 us
  Pallas kernels: 0 us -> 24.2 us
  between operations: 13.4 us -> 0.02 us
  matrix products: 5.39 us -> 0 us
  local copies, waits for them, and re-layouts: 9.69 us -> 4.93 us
  other arithmetic: 1.8 us -> 0 us
    all_gather x1 -> x0, waiting for transfers between devices: 43.2 us -> none  [local_xla(): whole = lax.all_gather(bank, ('shard', 'blk'), axis=0, tiled=True)]
    pallas_call x0 -> x1, Pallas kernels: none -> 24.2 us  [local_kernel(): pl.pallas_call(functools.partial(kernel, depth), out_shape=jax.ShapeDtype...]
    dot_general x3 -> x0, matrix products: 5.39 us -> none  [the longest x1 2.65 us: step(): jnp.einsum('thd,srhd->htsr', heads, keys, preferred_element_type=jnp.floa...]
    squeeze x1 -> x0, local copies, waits for them, and re-layouts: 4.36 us -> none  [local_xla(): lax.scan(step, start, blocked.transpose(1, 0, 2, 3, 4))]
    reduce_sum x1 -> x0, other arithmetic: 1.09 us -> none  [step(): total = total_old * factor + jnp.sum(weights, axis=(2, 3))]
    reshape x1 -> x0, local copies, waits for them, and re-layouts: 0.85 us -> none  [local_xla(): return out.transpose(1, 0, 2).reshape(rows, HEADS * HEAD_DIM)]
    unnamed x6 -> x8, local copies, waits for them, and re-layouts: 4.48 us -> 4.93 us
  transfers between devices with their start and end apart: 1 -> 0, of which waited for: 1 -> 0; matrix products, arithmetic and copies ran while one was open for 3% -> 0% of each run, Pallas kernels for 0% -> 0%
where the time goes in v2:
time: 29.4 us; the launch traced here: 29.2 us
  Pallas kernels  24.2 us (82%)
  local copies, waits for them, and re-layouts  4.93 us (17%)
    pallas_call x1, Pallas kernels, local_kernel(): pl.pallas_call(functools.partial(kernel, depth), out_shape=jax.ShapeDtype...  24.2 us
    unnamed x8, local copies, waits for them, and re-layouts  4.93 us

profile of v2, /device:TPU:1, one launch (start us, length us, event | category | flops | bytes accessed | tf_op | source)
XLA Modules:
  0.0 29.2 jit_solution(9490635462702754533)
XLA Ops:
  0.0 0.8 %copy.5.uses_ref = s32[128,2]{1,0:T(8,128)S(1)} copy(s32[128,2]{0,1:T(2,128)} %param.7) | data formatting | bytes 2048 | tf_op args[3]
  0.8 0.0 copy-start
  0.8 1.6 %copy-done = bf16[1024,1024]{1,0:T(8,128)(2,1)S(1)} copy-done((bf16[1024,1024]{1,0:T(8,128)(2,1)S(1)}, bf16[1024,1024]{1,0:T(8,128)(2,1)}, u32[]{:S(2)}) %copy-start) | copy-done | bytes 2097176
  2.4 0.0 copy-start.1
  2.4 0.9 %copy-done.1 = bf16[128,1024]{1,0:T(8,128)(2,1)S(1)} copy-done((bf16[128,1024]{1,0:T(8,128)(2,1)S(1)}, bf16[128,1024]{1,0:T(8,128)(2,1)}, u32[]{:S(2)}) %copy-start.1) | copy-done | bytes 262168
  3.3 0.0 copy-start.2
  3.3 0.9 %copy-done.2 = bf16[64,1024]{1,0:T(8,128)(2,1)S(1)} copy-done((bf16[64,1024]{1,0:T(8,128)(2,1)S(1)}, bf16[64,1024]{1,0:T(8,128)(2,1)}, u32[]{:S(2)}) %copy-start.2) | copy-done | bytes 131096
  4.2 24.2 %gather_attend.1 = bf16[128,1024]{1,0:T(8,128)(2,1)S(1)} custom-call(bf16[128,1024]{1,0:T(8,128)(2,1)S(1)} %copy-done.1, bf16[1024,1024]{1,0:T(8,128)(2,1)S(1)} %copy-done, bf16[64,1024]{1,0:T(8,128)(2,1)S(1)} %copy-done.2, s32[128,2]{1,0:T(8,128)S(1)} %copy.5.uses_ref), custom_call_target="tpu_custom_call" | custom-call | tf_op jit(solution)/shard_map/gather_attend/pallas_call | solution.py:190
  28.5 0.7 %copy.7 = bf16[128,1024]{1,0:T(8,128)(2,1)} copy(bf16[128,1024]{1,0:T(8,128)(2,1)S(1)} %gather_attend.1) | data formatting | bytes 524288
Async XLA Ops:
  0.8 1.6 %copy-start = (bf16[1024,1024]{1,0:T(8,128)(2,1)S(1)}, bf16[1024,1024]{1,0:T(8,128)(2,1)}, u32[]{:S(2)}) copy-start(bf16[1024,1024]{1,0:T(8,128)(2,1)} %weight_hbm.1) | copy-start | bytes 6291460
  2.4 0.9 %copy-start.1 = (bf16[128,1024]{1,0:T(8,128)(2,1)S(1)}, bf16[128,1024]{1,0:T(8,128)(2,1)}, u32[]{:S(2)}) copy-start(bf16[128,1024]{1,0:T(8,128)(2,1)} %queries_hbm.1) | copy-start | bytes 786436
  3.3 0.9 %copy-start.2 = (bf16[64,1024]{1,0:T(8,128)(2,1)S(1)}, bf16[64,1024]{1,0:T(8,128)(2,1)}, u32[]{:S(2)}) copy-start(bf16[64,1024]{1,0:T(8,128)(2,1)} %bank_hbm.1) | copy-start | bytes 393220

commit v3 on v2

--- a/solution.py
+++ b/solution.py
@@ -12,6 +12,7 @@
 HEAD_DIM = 128
 NEGATIVE = -1e30
 ALONG_X = 2
+PIECES = 2
 MESH = pl.DeviceIdType.MESH
 
 
@@ -29,6 +30,7 @@
     top_ref,
     total_ref,
     accum_ref,
+    masks,
     load_sems,
     z_sems,
     x_sems,
@@ -44,33 +46,42 @@
     def at(to_core, to_z, to_x):
         return (part, to_core, to_z * ALONG_X + to_x)
 
-    def copy(of_z, of_core, of_x, sems, target, source=None):
-        slot = held.at[of_z, of_core, of_x]
+    bank_rows = bank_hbm.shape[0] // PIECES
+
+    def copy(of_z, of_core, of_x, piece, sems, target, own=False):
+        slot = held.at[of_z, of_core, of_x, piece]
         return pltpu.make_async_remote_copy(
-            src_ref=slot if source is None else source,
+            src_ref=bank_hbm.at[pl.ds(piece * bank_rows, bank_rows)] if own else slot,
             dst_ref=slot,
-            send_sem=sems.at[of_z, of_x],
-            recv_sem=recv_sems.at[of_z, of_core, of_x],
+            send_sem=sems.at[of_z, of_x, piece],
+            recv_sem=recv_sems.at[of_z, of_core, of_x, piece],
             device_id=target,
             device_id_type=MESH,
         )
 
-    def along(of_z, step, source=None):
-        return copy(of_z, core, x, z_sems.at[0 if step > 0 else 1], at(core, z + step, x), source)
-
-    def across(of_z, source=None):
-        return copy(of_z, core, x, x_sems, at(core, z, other_x), source)
-
-    def over(of_z, of_x, source=None):
-        return copy(of_z, core, of_x, core_sems, at(other_core, z, x), source)
-
-    def arrived(of_z, of_core, of_x):
-        copy(of_z, of_core, of_x, x_sems, at(core, z, other_x)).wait_recv()
+    def along(of_z, piece, step, own=False):
+        sems = z_sems.at[0 if step > 0 else 1]
+        return copy(of_z, core, x, piece, sems, at(core, z + step, x), own)
+
+    def across(of_z, piece, own=False):
+        return copy(of_z, core, x, piece, x_sems, at(core, z, other_x), own)
+
+    def over(of_z, of_x, piece, own=False):
+        return copy(of_z, core, of_x, piece, core_sems, at(other_core, z, x), own)
+
+    def arrived(of_z, of_core, of_x, piece):
+        copy(of_z, of_core, of_x, piece, x_sems, at(core, z, other_x)).wait_recv()
 
     loads = [
         pltpu.make_async_copy(weight_hbm, weight_ref, load_sems.at[0]),
         pltpu.make_async_copy(queries_hbm, queries_ref, load_sems.at[1]),
-        pltpu.make_async_copy(bank_hbm, held.at[z, core, x], load_sems.at[2]),
+    ] + [
+        pltpu.make_async_copy(
+            bank_hbm.at[pl.ds(piece * bank_rows, bank_rows)],
+            held.at[z, core, x, piece],
+            load_sems.at[2 + piece],
+        )
+        for piece in range(PIECES)
     ]
     for load in loads:
         load.start()
@@ -87,10 +98,12 @@
     pl.when(above)(lambda: greet(at(core, z + 1, x)))
     pl.semaphore_wait(barrier, 2 + below.astype(jnp.int32) + above.astype(jnp.int32))
 
-    pl.when(below)(lambda: along(z, -1, bank_hbm).start())
-    pl.when(above)(lambda: along(z, 1, bank_hbm).start())
-    across(z, bank_hbm).start()
-    over(z, x, bank_hbm).start()
+    for piece in range(PIECES):
+        pl.when(below)(lambda piece=piece: along(z, piece, -1, True).start())
+        pl.when(above)(lambda piece=piece: along(z, piece, 1, True).start())
+        across(z, piece, True).start()
+    for piece in range(PIECES):
+        over(z, x, piece, True).start()
 
     for load in loads[:2]:
         load.wait()
@@ -99,21 +112,23 @@
         projected[:, columns] = jnp.dot(
             queries_ref[...], weight_ref[:, columns], preferred_element_type=jnp.float32
         ).astype(jnp.bfloat16)
-    loads[2].wait()
+    for load in loads[2:]:
+        load.wait()
+    for shard in range(2):
+        listed = uses_ref[shard : shard + 1, :].astype(jnp.float32)
+        masks[shard] = jnp.broadcast_to(listed, (HEAD_DIM, listed.shape[1])).T
 
     factor = HEAD_DIM**-0.5 * math.log2(math.e)
-    rows = held.shape[3]
+    rows = bank_hbm.shape[0]
     plane_rows = 2 * ALONG_X * rows
     rows_q = projected.shape[0]
 
     def attend(of_z, first):
-        in_second = (
-            lax.broadcasted_iota(jnp.int32, (rows_q, plane_rows), 1) >= ALONG_X * rows
-        )
-        allowed = jnp.where(in_second, uses_ref[:, 1:2], uses_ref[:, 0:1]) > 0
+        repeats = ALONG_X * rows // HEAD_DIM
+        allowed = jnp.concatenate([masks[0]] * repeats + [masks[1]] * repeats, axis=1) > 0.5
         for head in range(HEADS):
             columns = slice(head * HEAD_DIM, (head + 1) * HEAD_DIM)
-            keys = held[of_z, :, :, :, columns].reshape(plane_rows, HEAD_DIM)
+            keys = held[of_z, :, :, :, :, columns].reshape(plane_rows, HEAD_DIM)
             scores = lax.dot_general(
                 projected[:, columns],
                 keys,
@@ -150,18 +165,23 @@
         pl.when(z < depth - distance)(lambda: action(z + distance, -1))
 
     def relay(of_z, step):
-        arrived(of_z, core, x)
-        pl.when((z + step >= 0) & (z + step < depth))(lambda: along(of_z, step).start())
-        across(of_z).start()
-        over(of_z, x).start()
+        for piece in range(PIECES):
+            arrived(of_z, core, x, piece)
+            pl.when((z + step >= 0) & (z + step < depth))(
+                lambda piece=piece: along(of_z, piece, step).start()
+            )
+            across(of_z, piece).start()
+            over(of_z, x, piece).start()
 
     def hand_over(of_z, step):
-        arrived(of_z, core, other_x)
-        over(of_z, other_x).start()
+        for piece in range(PIECES):
+            arrived(of_z, core, other_x, piece)
+            over(of_z, other_x, piece).start()
 
     def finish_plane(of_z, step):
-        arrived(of_z, other_core, 0)
-        arrived(of_z, other_core, 1)
+        for of_x in range(ALONG_X):
+            for piece in range(PIECES):
+                arrived(of_z, other_core, of_x, piece)
         attend(of_z, step == 0)
 
     for distance in range(depth):
@@ -175,42 +195,47 @@
         total = jnp.sum(total_ref[head], axis=1, keepdims=True)
         out_ref[:, columns] = (accum_ref[head] / total).astype(out_ref.dtype)
 
+    def drain(of_z, piece):
+        pl.when((z >= of_z) & above)(lambda: along(of_z, piece, 1).wait_send())
+        pl.when((z <= of_z) & below)(lambda: along(of_z, piece, -1).wait_send())
+        across(of_z, piece).wait_send()
+        for of_x in range(ALONG_X):
+            over(of_z, of_x, piece).wait_send()
+
     for of_z in range(depth):
-        pl.when((z >= of_z) & above)(lambda of_z=of_z: along(of_z, 1).wait_send())
-        pl.when((z <= of_z) & below)(lambda of_z=of_z: along(of_z, -1).wait_send())
-        across(of_z).wait_send()
-        for of_x in range(ALONG_X):
-            over(of_z, of_x).wait_send()
+        for piece in range(PIECES):
+            drain(of_z, piece)
 
 
 def local_kernel(depth, queries_in, query_weight, bank, uses):
     rows_q, width = queries_in.shape
     rows = bank.shape[0]
-    any_space = pl.BlockSpec(memory_space=pl.ANY)
+    any_space = pl.BlockSpec(memory_space=pltpu.HBM)
     return pl.pallas_call(
         functools.partial(kernel, depth),
         out_shape=jax.ShapeDtypeStruct((rows_q, HEADS * HEAD_DIM), jnp.bfloat16),
         in_specs=[any_space, any_space, any_space, pl.BlockSpec(memory_space=pltpu.VMEM)],
         out_specs=pl.BlockSpec(memory_space=pltpu.VMEM),
         scratch_shapes=[
-            pltpu.VMEM((depth, 2, ALONG_X, rows, width), jnp.bfloat16),
+            pltpu.VMEM((depth, 2, ALONG_X, PIECES, rows // PIECES, width), jnp.bfloat16),
             pltpu.VMEM((rows_q, width), jnp.bfloat16),
             pltpu.VMEM((width, width), jnp.bfloat16),
             pltpu.VMEM((rows_q, width), jnp.bfloat16),
             pltpu.VMEM((HEADS, rows_q, HEAD_DIM), jnp.float32),
             pltpu.VMEM((HEADS, rows_q, HEAD_DIM), jnp.float32),
             pltpu.VMEM((HEADS, rows_q, HEAD_DIM), jnp.float32),
-            pltpu.SemaphoreType.DMA((3,)),
-            pltpu.SemaphoreType.DMA((2, depth, ALONG_X)),
-            pltpu.SemaphoreType.DMA((depth, ALONG_X)),
-            pltpu.SemaphoreType.DMA((depth, ALONG_X)),
-            pltpu.SemaphoreType.DMA((depth, 2, ALONG_X)),
+            pltpu.VMEM((2, rows_q, HEAD_DIM), jnp.float32),
+            pltpu.SemaphoreType.DMA((2 + PIECES,)),
+            pltpu.SemaphoreType.DMA((2, depth, ALONG_X, PIECES)),
+            pltpu.SemaphoreType.DMA((depth, ALONG_X, PIECES)),
+            pltpu.SemaphoreType.DMA((depth, ALONG_X, PIECES)),
+            pltpu.SemaphoreType.DMA((depth, 2, ALONG_X, PIECES)),
         ],
         compiler_params=pltpu.CompilerParams(
-            collective_id=0, has_side_effects=True, vmem_limit_bytes=32 * 2**20
+            collective_id=0, has_side_effects=True, vmem_limit_bytes=56 * 2**20
         ),
         name="gather_attend",
-    )(queries_in, query_weight, bank, uses)
+    )(queries_in, query_weight, bank, uses.T)
 
 
 def local_xla(queries_in, query_weight, bank, uses):

time: 29.4 us -> 26.7 us (0.908)
  local copies, waits for them, and re-layouts: 4.93 us -> 1.67 us
  Pallas kernels: 24.2 us -> 24.9 us
    unnamed x8 -> x1, local copies, waits for them, and re-layouts: 4.93 us -> 1.67 us
    pallas_call x1, Pallas kernels: 24.2 us -> 24.9 us  [local_kernel(): pl.pallas_call(functools.partial(kernel, depth), out_shape=jax.ShapeDtype...]
where the time goes in v3:
time: 26.7 us; the launch traced here: 26.6 us
  Pallas kernels  24.9 us (93%)
  local copies, waits for them, and re-layouts  1.67 us (6%)
    pallas_call x1, Pallas kernels, local_kernel(): pl.pallas_call(functools.partial(kernel, depth), out_shape=jax.ShapeDtype...  24.9 us
    unnamed x1, local copies, waits for them, and re-layouts  1.67 us

profile of v3, /device:TPU:1, one launch (start us, length us, event | category | flops | bytes accessed | tf_op | source)
XLA Modules:
  0.0 26.6 jit_solution(444260568188886325)
XLA Ops:
  0.0 24.9 %gather_attend.1 = bf16[128,1024]{1,0:T(8,128)(2,1)} custom-call(bf16[128,1024]{1,0:T(8,128)(2,1)} %queries_hbm.1, bf16[1024,1024]{1,0:T(8,128)(2,1)} %weight_hbm.1, bf16[64,1024]{1,0:T(8,128)(2,1)} %bank_hbm.1, s32[2,128]{1,0:T(2,128)} %bitcast.1), custom_call_target="tpu_custom_call" | custom-call | tf_op jit(solution)/shard_map/gather_attend/pallas_call | solution.py:214
  24.9 1.7 %copy.6 = bf16[128,1024]{1,0:T(8,128)(2,1)} copy(bf16[128,1024]{1,0:T(8,128)(2,1)} %gather_attend.1) | data formatting | bytes 524288

commit v4 on v3

--- a/solution.py
+++ b/solution.py
@@ -48,10 +48,10 @@
 
     bank_rows = bank_hbm.shape[0] // PIECES
 
-    def copy(of_z, of_core, of_x, piece, sems, target, own=False):
+    def copy(of_z, of_core, of_x, piece, sems, target):
         slot = held.at[of_z, of_core, of_x, piece]
         return pltpu.make_async_remote_copy(
-            src_ref=bank_hbm.at[pl.ds(piece * bank_rows, bank_rows)] if own else slot,
+            src_ref=slot,
             dst_ref=slot,
             send_sem=sems.at[of_z, of_x, piece],
             recv_sem=recv_sems.at[of_z, of_core, of_x, piece],
@@ -59,15 +59,15 @@
             device_id_type=MESH,
         )
 
-    def along(of_z, piece, step, own=False):
+    def along(of_z, piece, step):
         sems = z_sems.at[0 if step > 0 else 1]
-        return copy(of_z, core, x, piece, sems, at(core, z + step, x), own)
-
-    def across(of_z, piece, own=False):
-        return copy(of_z, core, x, piece, x_sems, at(core, z, other_x), own)
-
-    def over(of_z, of_x, piece, own=False):
-        return copy(of_z, core, of_x, piece, core_sems, at(other_core, z, x), own)
+        return copy(of_z, core, x, piece, sems, at(core, z + step, x))
+
+    def across(of_z, piece):
+        return copy(of_z, core, x, piece, x_sems, at(core, z, other_x))
+
+    def over(of_z, of_x, piece):
+        return copy(of_z, core, of_x, piece, core_sems, at(other_core, z, x))
 
     def arrived(of_z, of_core, of_x, piece):
         copy(of_z, of_core, of_x, piece, x_sems, at(core, z, other_x)).wait_recv()
@@ -83,7 +83,7 @@
         )
         for piece in range(PIECES)
     ]
-    for load in loads:
+    for load in loads[2:]:
         load.start()
 
     barrier = pltpu.get_barrier_semaphore()
@@ -98,12 +98,16 @@
     pl.when(above)(lambda: greet(at(core, z + 1, x)))
     pl.semaphore_wait(barrier, 2 + below.astype(jnp.int32) + above.astype(jnp.int32))
 
+    for load in loads[2:]:
+        load.wait()
     for piece in range(PIECES):
-        pl.when(below)(lambda piece=piece: along(z, piece, -1, True).start())
-        pl.when(above)(lambda piece=piece: along(z, piece, 1, True).start())
-        across(z, piece, True).start()
+        pl.when(below)(lambda piece=piece: along(z, piece, -1).start())
+        pl.when(above)(lambda piece=piece: along(z, piece, 1).start())
+        across(z, piece).start()
     for piece in range(PIECES):
-        over(z, x, piece, True).start()
+        over(z, x, piece).start()
+    for load in loads[:2]:
+        load.start()
 
     for load in loads[:2]:
         load.wait()
@@ -112,8 +116,6 @@
         projected[:, columns] = jnp.dot(
             queries_ref[...], weight_ref[:, columns], preferred_element_type=jnp.float32
         ).astype(jnp.bfloat16)
-    for load in loads[2:]:
-        load.wait()
     for shard in range(2):
         listed = uses_ref[shard : shard + 1, :].astype(jnp.float32)
         masks[shard] = jnp.broadcast_to(listed, (HEAD_DIM, listed.shape[1])).T

time: 26.7 us -> 26.4 us (0.989)
  Pallas kernels: 24.9 us -> 24.6 us
    pallas_call x1, Pallas kernels: 24.9 us -> 24.6 us  [local_kernel(): pl.pallas_call(functools.partial(kernel, depth), out_shape=jax.ShapeDtype...]
where the time goes in v4:
time: 26.4 us; the launch traced here: 26.2 us
  Pallas kernels  24.6 us (93%)
  local copies, waits for them, and re-layouts  1.67 us (6%)
    pallas_call x1, Pallas kernels, local_kernel(): pl.pallas_call(functools.partial(kernel, depth), out_shape=jax.ShapeDtype...  24.6 us
    unnamed x1, local copies, waits for them, and re-layouts  1.67 us

profile of v4, /device:TPU:1, one launch (start us, length us, event | category | flops | bytes accessed | tf_op | source)
XLA Modules:
  0.0 26.2 jit_solution(5098899393827242995)
XLA Ops:
  0.0 24.6 %gather_attend.1 = bf16[128,1024]{1,0:T(8,128)(2,1)} custom-call(bf16[128,1024]{1,0:T(8,128)(2,1)} %queries_hbm.1, bf16[1024,1024]{1,0:T(8,128)(2,1)} %weight_hbm.1, bf16[64,1024]{1,0:T(8,128)(2,1)} %bank_hbm.1, s32[2,128]{1,0:T(2,128)} %bitcast.1), custom_call_target="tpu_custom_call" | custom-call | tf_op jit(solution)/shard_map/gather_attend/pallas_call | solution.py:216
  24.6 1.7 %copy.6 = bf16[128,1024]{1,0:T(8,128)(2,1)} copy(bf16[128,1024]{1,0:T(8,128)(2,1)} %gather_attend.1) | data formatting | bytes 524288

commit v5 on v4

--- a/solution.py
+++ b/solution.py
@@ -103,22 +103,12 @@
     for piece in range(PIECES):
         pl.when(below)(lambda piece=piece: along(z, piece, -1).start())
         pl.when(above)(lambda piece=piece: along(z, piece, 1).start())
+    for piece in range(PIECES):
         across(z, piece).start()
     for piece in range(PIECES):
         over(z, x, piece).start()
     for load in loads[:2]:
         load.start()
-
-    for load in loads[:2]:
-        load.wait()
-    for head in range(0, HEADS, 2):
-        columns = slice(head * HEAD_DIM, (head + 2) * HEAD_DIM)
-        projected[:, columns] = jnp.dot(
-            queries_ref[...], weight_ref[:, columns], preferred_element_type=jnp.float32
-        ).astype(jnp.bfloat16)
-    for shard in range(2):
-        listed = uses_ref[shard : shard + 1, :].astype(jnp.float32)
-        masks[shard] = jnp.broadcast_to(listed, (HEAD_DIM, listed.shape[1])).T
 
     factor = HEAD_DIM**-0.5 * math.log2(math.e)
     rows = bank_hbm.shape[0]
@@ -159,6 +149,18 @@
             total_ref[head] = total
             accum_ref[head] = summed
 
+    def project():
+        for load in loads[:2]:
+            load.wait()
+        for head in range(0, HEADS, 2):
+            columns = slice(head * HEAD_DIM, (head + 2) * HEAD_DIM)
+            projected[:, columns] = jnp.dot(
+                queries_ref[...], weight_ref[:, columns], preferred_element_type=jnp.float32
+            ).astype(jnp.bfloat16)
+        for shard in range(2):
+            listed = uses_ref[shard : shard + 1, :].astype(jnp.float32)
+            masks[shard] = jnp.broadcast_to(listed, (HEAD_DIM, listed.shape[1])).T
+
     def planes(distance, action):
         if distance == 0:
             action(z, 0)
@@ -190,6 +192,8 @@
         if distance + 1 < depth:
             planes(distance + 1, relay)
         planes(distance, hand_over)
+        if distance == 0:
+            project()
         planes(distance, finish_plane)
 
     for head in range(HEADS):

time: 26.4 us -> 26.4 us (level)
  no operation moved by 1% of the time
where the time goes in v5:
time: 26.4 us; the launch traced here: 26.3 us
  Pallas kernels  24.6 us (93%)
  local copies, waits for them, and re-layouts  1.67 us (6%)
    pallas_call x1, Pallas kernels, local_kernel(): pl.pallas_call(functools.partial(kernel, depth), out_shape=jax.ShapeDtype...  24.6 us
    unnamed x1, local copies, waits for them, and re-layouts  1.67 us

profile of v5, /device:TPU:1, one launch (start us, length us, event | category | flops | bytes accessed | tf_op | source)
XLA Modules:
  0.0 26.3 jit_solution(7438675105526723000)
XLA Ops:
  0.0 24.6 %gather_attend.1 = bf16[128,1024]{1,0:T(8,128)(2,1)} custom-call(bf16[128,1024]{1,0:T(8,128)(2,1)} %queries_hbm.1, bf16[1024,1024]{1,0:T(8,128)(2,1)} %weight_hbm.1, bf16[64,1024]{1,0:T(8,128)(2,1)} %bank_hbm.1, s32[2,128]{1,0:T(2,128)} %bitcast.1), custom_call_target="tpu_custom_call" | custom-call | tf_op jit(solution)/shard_map/gather_attend/pallas_call | solution.py:220
  24.6 1.7 %copy.6 = bf16[128,1024]{1,0:T(8,128)(2,1)} copy(bf16[128,1024]{1,0:T(8,128)(2,1)} %gather_attend.1) | data formatting | bytes 524288
